TPU v7x, 32 devices: a whole 2x2x4 slice. The times are simulated.
32 devices in a mesh: geom: 2 (over x), aux: 16 (over z, y, core).
Axes of the slice: x: 2, y: 2, z: 4, core: 2. Of those that a mesh axis runs over, the one named last changes fastest.
Arguments:
- trial_vecs: float32 [8, 128, 224], P('geom', 'aux'), parts along dimension 0, may hold values from -6 to 6
- occ_energy: float32 [256], P('geom'), parts along dimension 0, may hold values from -1.5 to -0.2
- vir_energy: float32 [448], P('geom'), parts along dimension 0, may hold values from 0.2 to 2.5
- coul_ov: bfloat16 [2048, 128, 224], P(('geom', 'aux')), parts along dimension 0, may hold values from -0.03125 to 0.03125
- exch_oo: bfloat16 [2048, 128, 128], P(('geom', 'aux')), parts along dimension 0, may hold values from -0.0234375 to 0.0234375
- exch_vv: bfloat16 [2048, 224, 224], P(('geom', 'aux')), parts along dimension 0, may hold values from -0.375 to 0.375
Outputs:
- sigma_vecs: float32 [8, 128, 224], P('geom', 'aux'), parts along dimension 0
- update_vecs: float32 [8, 128, 224], P('geom', 'aux'), parts along dimension 0
There are 2 independent parts, one for each index of `geom`. A program takes and returns all parts, laid end to end along the dimension named above; each array names one. Nothing has to cross between parts.
All inputs are finite; a program needn't handle non-finite values.
Results may differ from a plain program's by a relative error of at most 0.0037.
Values may be sent and summed in bfloat16 or wider, within the bound.
A program may use at most 64 MiB of HBM per device.

v0:
```python
import math

import jax
import jax.numpy as jnp
from jax import lax
from jax.sharding import PartitionSpec as P


def contract(totals, rows_x, coul_ov, exch_oo, exch_vv):
    aux_coef, exchange = totals
    height = rows_x.shape[1]
    n_occ = exch_oo.shape[1]
    n_virt = exch_vv.shape[1]
    aux_coef = jnp.einsum("pia,nia->np", coul_ov, rows_x, preferred_element_type=jnp.float32)
    aux_local = exch_vv.shape[0]
    group_size = math.gcd(aux_local, 16)
    group_count = aux_local // group_size
    vv_groups = exch_vv.reshape(group_count, group_size, n_virt, n_virt)
    oo_groups = exch_oo.reshape(group_count, group_size, n_occ, height)

    def advance(running, parts_pair):
        vv_part, oo_part = parts_pair
        halfway = jnp.einsum(
            "pab,njb->pnja", vv_part, rows_x, preferred_element_type=jnp.float32
        ).astype(jnp.bfloat16)
        return (
            running
            + jnp.einsum("pij,pnja->nia", oo_part, halfway, preferred_element_type=jnp.float32),
            None,
        )

    exchange, _ = lax.scan(advance, exchange, (vv_groups, oo_groups))
    return (aux_coef, exchange)


def residual_step(sigma_part, trial_part, diagonal, omega):
    resid = sigma_part - omega[:, None, None] * trial_part
    gap = jnp.maximum(jnp.abs(diagonal[None] - omega[:, None, None]), 1.0)
    return resid / gap


def on_device(trial_vecs, occ_energy, vir_energy, coul_ov, exch_oo, exch_vv):
    n_trial = trial_vecs.shape[0]
    local_rows = trial_vecs.shape[1]
    n_virt = trial_vecs.shape[2]
    n_occ = exch_oo.shape[1]
    aux_local = coul_ov.shape[0]
    empty = (
        jnp.zeros((n_trial, aux_local), jnp.float32),
        jnp.zeros((n_trial, n_occ, n_virt), jnp.float32),
    )
    row_start = lax.axis_index("aux") * local_rows
    wide_x = lax.all_gather(trial_vecs, "aux", axis=1, tiled=True)
    aux_coef, exchange = contract(empty, wide_x.astype(jnp.bfloat16), coul_ov, exch_oo, exch_vv)
    coulomb = jnp.einsum(
        "pia,np->nia", coul_ov, aux_coef.astype(jnp.bfloat16), preferred_element_type=jnp.float32
    )
    summed = lax.psum(2.0 * coulomb - exchange, "aux")
    diagonal = vir_energy[None, :] - occ_energy[:, None]
    sigma_all = diagonal[None] * wide_x + summed
    omega = jnp.sum(wide_x * sigma_all, axis=(1, 2)) / (
        jnp.sum(wide_x * wide_x, axis=(1, 2)) + 1e-06
    )
    precond = residual_step(sigma_all, wide_x, diagonal, omega)
    update_all = (
        precond * lax.rsqrt(jnp.mean(precond * precond, axis=(1, 2)) + 1e-06)[:, None, None]
    )
    sigma_vecs = lax.dynamic_slice_in_dim(sigma_all, row_start, local_rows, 1)
    update_vecs = lax.dynamic_slice_in_dim(update_all, row_start, local_rows, 1)
    return (sigma_vecs, update_vecs)


def solution(mesh):
    in_specs = (
        P("geom", "aux", None),
        P("geom"),
        P("geom"),
        P(("geom", "aux"), None, None),
        P(("geom", "aux"), None, None),
        P(("geom", "aux"), None, None),
    )
    out_specs = (P("geom", "aux", None), P("geom", "aux", None))
    return jax.shard_map(
        on_device, mesh=mesh, in_specs=in_specs, out_specs=out_specs, check_vma=False
    )
```

profile of v0, /device:TPU:0, one launch (start us, length us, event | category | flops | bytes accessed | tf_op | source)
XLA Modules:
  0.0 159.7 jit_solution(4688570363606826687)
XLA Ops:
  7.2 0.0 all-reduce.2.cloned.1.call-start
  7.2 0.8 copy.23
  8.0 24.6 %all_gather.3 = f32[4,128,224]{2,0,1:T(4,128)S(1)} all-gather(f32[4,8,224]{2,0,1:T(4,128)S(1)} %copy.23), channel_id=1, replica_groups=mesh['geom'=2,'aux'=16] {'aux'}, dimensions={1}, use_global_device_ids=true | all-gather | bytes 487424 | tf_op jit(solution)/shard_map/all_gather | solution.py:53
  32.6 0.4 multiply_reduce_fusion
  33.0 6.8 %copy.25 = bf16[64,128,224]{2,0,1:T(8,128)(2,1)} copy(bf16[64,128,224]{1,2,0:T(8,128)(2,1)} %param.11) | data formatting | bytes 7340032 | tf_op args[3]
  39.7 0.2 copy.28
  40.0 6.1 %fusion.25 = f32[4,128,224]{1,0,2:T(4,128)S(1)} fusion(bf16[64,128,224]{1,2,0:T(8,128)(2,1)} %param.11, bf16[4,128,224]{2,0,1:T(4,128)(2,1)S(1)} %get-tuple-element.84, bf16[64,128,224]{2,0,1:T(8,128)(2,1)} %copy.25), kind=kOutput, calls=%fused_computation.12 | convolution fusion | flops 29360384 | bytes 8028160 | tf_op jit(solution)/shard_map/pia,np->nia/dot_general | solution.py:55
  46.1 0.0 copy-start
  46.1 0.0 copy-start.1
  46.1 15.2 %while.11 = (s32[]{:T(128)}, f32[4,128,224]{1,2,0:T(8,128)S(1)}, bf16[4,16,224,224]{3,2,1,0:T(8,128)(2,1)}, bf16[4,128,224]{1,2,0:T(8,128)(2,1)S(1)}, bf16[4,16,...) while((s32[]{:T(128)}, f32[4,128,224]{1,2,0:T(8,128)S(1)}, ...), condition=%wide.region_1.2_spmd.clone, body=%wide.region_0.1_spmd.clone.sunk | while | flops 1293910016 | bytes 3507287 | solution.py:32
  46.1 3.8 %fusion.41 = f32[4,128,224]{1,2,0:T(8,128)S(1)} fusion(bf16[4,16,224,224]{3,2,1,0:T(8,128)(2,1)} %get-tuple-element.134, s32[]{:T(128)} %get-tuple-element.125, bf16[4,16,128,128]{3,2,1,0:T(8,128)(2,1)} %get-tuple-element.136, f32[4,128,224]{1,2,0:T(8,128)S(1)} %get-tuple-element.126, bf16[4,128,224]{1,2,0:T(8,128)(2,1)S(1)} %get-tuple-element.135, ...), kind=kOutput, calls=%fused_computation.7.clone.1 | convolution fusion | flops 1293910016 | bytes 3507201 | tf_op jit(solution)/shard_map/while/body/eval_jaxpr/pij,pnja->nia/dot_general | solution.py:28
  49.9 3.8 %fusion.41 = f32[4,128,224]{1,2,0:T(8,128)S(1)} fusion(bf16[4,16,224,224]{3,2,1,0:T(8,128)(2,1)} %get-tuple-element.134, s32[]{:T(128)} %get-tuple-element.125, bf16[4,16,128,128]{3,2,1,0:T(8,128)(2,1)} %get-tuple-element.136, f32[4,128,224]{1,2,0:T(8,128)S(1)} %get-tuple-element.126, bf16[4,128,224]{1,2,0:T(8,128)(2,1)S(1)} %get-tuple-element.135, ...), kind=kOutput, calls=%fused_computation.7.clone.1 | convolution fusion | flops 1293910016 | bytes 3507201 | tf_op jit(solution)/shard_map/while/body/eval_jaxpr/pij,pnja->nia/dot_general | solution.py:28
  53.7 3.8 %fusion.41 = f32[4,128,224]{1,2,0:T(8,128)S(1)} fusion(bf16[4,16,224,224]{3,2,1,0:T(8,128)(2,1)} %get-tuple-element.134, s32[]{:T(128)} %get-tuple-element.125, bf16[4,16,128,128]{3,2,1,0:T(8,128)(2,1)} %get-tuple-element.136, f32[4,128,224]{1,2,0:T(8,128)S(1)} %get-tuple-element.126, bf16[4,128,224]{1,2,0:T(8,128)(2,1)S(1)} %get-tuple-element.135, ...), kind=kOutput, calls=%fused_computation.7.clone.1 | convolution fusion | flops 1293910016 | bytes 3507201 | tf_op jit(solution)/shard_map/while/body/eval_jaxpr/pij,pnja->nia/dot_general | solution.py:28
  57.5 3.8 %fusion.41 = f32[4,128,224]{1,2,0:T(8,128)S(1)} fusion(bf16[4,16,224,224]{3,2,1,0:T(8,128)(2,1)} %get-tuple-element.134, s32[]{:T(128)} %get-tuple-element.125, bf16[4,16,128,128]{3,2,1,0:T(8,128)(2,1)} %get-tuple-element.136, f32[4,128,224]{1,2,0:T(8,128)S(1)} %get-tuple-element.126, bf16[4,128,224]{1,2,0:T(8,128)(2,1)S(1)} %get-tuple-element.135, ...), kind=kOutput, calls=%fused_computation.7.clone.1 | convolution fusion | flops 1293910016 | bytes 3507201 | tf_op jit(solution)/shard_map/while/body/eval_jaxpr/pij,pnja->nia/dot_general | solution.py:28
  61.3 0.8 fusion.29
  62.1 0.0 all-reduce.2.cloned.1.call-update
  62.1 0.2 copy.24
  62.4 0.0 copy-done
  62.4 0.0 copy-done.1
  62.4 0.1 broadcast_subtract_fusion
  62.5 86.9 %all-reduce.2.cloned.1.call-done = f32[4,128,224]{1,2,0:T(8,128)} async-done(((f32[4,128,224]{1,2,0:T(8,128)}), f32[4,128,224]{1,2,0:T(8,128)}) %all-reduce.2.cloned.1.call-update) | async-done | bytes 458768 | tf_op jit(solution)/shard_map/psum | solution.py:58
  149.4 1.2 multiply_reduce_fusion.2
  150.6 0.3 multiply_reduce_fusion.1
  151.0 0.3 dynamic-slice_multiply_fusion
  151.3 0.8 copy.31
  152.1 0.8 copy.32
  (3 shorter events, 0.0 us)
Async XLA Ops:
  7.2 142.3 %all-reduce.2.cloned.1.call-start = ((), (), s32[]{:S(2)}) async-start(), calls=%async_computation | async-start | bytes 917504 | tf_op jit(solution)/shard_map/psum | solution.py:58
  46.1 16.3 %copy-start = (f32[224]{0:T(256)S(1)}, f32[224]{0:T(256)}, u32[]{:S(2)}) copy-start(f32[224]{0:T(256)} %param.10) | copy-start | bytes 2692
  46.1 16.3 %copy-start.1 = (f32[128]{0:T(128)S(1)}, f32[128]{0:T(128)}, u32[]{:S(2)}) copy-start(f32[128]{0:T(128)} %param.9) | copy-start | bytes 1540
Sparse Core Ops, SparseCore 0:
  62.3 87.1 all-reduce.1
where the time goes:
time: 160 us
  waiting for transfers between devices  87 us (54%)
  blocking collectives  24.6 us (15%)
  matrix products  21.2 us (13%)
  between operations  14.1 us (9%)
  local copies, waits for them, and re-layouts  9.57 us (6%)
  other arithmetic  3.17 us (2%)
    psum x1, waiting for transfers between devices, on_device(): summed = lax.psum(2.0 * coulomb - exchange, 'aux')  86.9 us
    all_gather x1, blocking collectives, on_device(): wide_x = lax.all_gather(trial_vecs, 'aux', axis=1, tiled=True)  24.6 us
    dot_general x4, matrix products, advance(): jnp.einsum('pij,pnja->nia', oo_part, halfway, preferred_element_type=jnp....  15.1 us
    unnamed x9, local copies, waits for them, and re-layouts  9.34 us
    dot_general x1, matrix products, on_device(): jnp.einsum('pia,np->nia', coul_ov, aux_coef.astype(jnp.bfloat16), preferr...  6.1 us
  transfers between devices with their start and end apart: 1, of which 1 were waited for; matrix products, arithmetic and copies ran while one was open for 0% of the time, Pallas kernels for 0%

commit v1 on v0

v1 whole, which is shorter than its diff:
```python
import functools
import math

import jax
import jax.numpy as jnp
from jax import lax
from jax.experimental import pallas as pl
from jax.experimental.pallas import tpu as pltpu
from jax.sharding import PartitionSpec as P

MESH = pl.DeviceIdType.MESH
NT_DIMS = (((1,), (1,)), ((), ()))


def sigma_kernel(
    n_dev,
    group,
    x_ref,
    occ_ref,
    vir_ref,
    coul_hbm,
    oo_hbm,
    vv_hbm,
    sigma_ref,
    update_ref,
    coul,
    oo,
    vv,
    x_pad,
    gathered,
    x_t,
    total,
    outgoing,
    incoming,
    scalars_out,
    scalars_in,
    norms_out,
    norms_in,
    load_sem,
    gather_send,
    gather_recv,
    sum_send,
    sum_recv,
    scalar_send,
    scalar_recv,
    norm_send,
    norm_recv,
):
    me = lax.axis_index("aux")
    n_trial, rows, n_virt = x_ref.shape
    aux_local, n_occ, _ = oo.shape
    width = x_pad.shape[1]
    half_trials = n_trial // 2
    half_cols = half_trials * n_occ
    f32, bf16 = jnp.float32, jnp.bfloat16

    loads = [
        pltpu.make_async_copy(source, target, load_sem.at[slot])
        for slot, (source, target) in enumerate(((coul_hbm, coul), (vv_hbm, vv), (oo_hbm, oo)))
    ]
    for load in loads:
        load.start()

    barrier = pltpu.get_barrier_semaphore()

    def greet(step, carry):
        pl.semaphore_signal(
            barrier, inc=1, device_id={"aux": lax.rem(me + step, n_dev)}, device_id_type=MESH
        )
        return carry

    lax.fori_loop(1, n_dev, greet, 0)

    x_pad[...] = jnp.zeros_like(x_pad)
    x_pad[:, :n_virt] = x_ref[...].reshape(n_trial * rows, n_virt)
    gathered[me] = x_pad[...].astype(bf16)
    pl.semaphore_wait(barrier, n_dev - 1)

    def to_peer(source, target, send_sem, recv_sem, step):
        return pltpu.make_async_remote_copy(
            src_ref=source,
            dst_ref=target,
            send_sem=send_sem.at[step],
            recv_sem=recv_sem.at[step],
            device_id={"aux": lax.rem(me + step, n_dev)},
            device_id_type=MESH,
        )

    def gather_copy(step):
        return to_peer(gathered.at[me], gathered.at[me], gather_send, gather_recv, step)

    def sum_copy(half, step):
        peer = lax.rem(me + step, n_dev)
        return to_peer(
            outgoing.at[half, peer], incoming.at[half, me], sum_send.at[half], sum_recv.at[half], step
        )

    def scalar_copy(step):
        return to_peer(scalars_out, scalars_in.at[me], scalar_send, scalar_recv, step)

    def norm_copy(step):
        return to_peer(norms_out, norms_in.at[me], norm_send, norm_recv, step)

    def each(action):
        def body(step, carry):
            action(step)
            return carry

        lax.fori_loop(1, n_dev, body, 0)

    each(lambda step: gather_copy(step).start())
    for load in loads:
        load.wait()
    each(lambda step: gather_copy(step).wait_recv())

    wide = gathered[...].astype(f32).reshape(n_dev, n_trial, rows, width)
    for n in range(n_trial):
        x_t[:, n * n_occ : (n + 1) * n_occ] = (
            wide[:, n].reshape(n_occ, width).T.astype(bf16)
        )

    block = 16
    pairs = n_virt // (2 * block)
    z_rows, z_cols = n_trial * block, aux_local * block

    def coul_block(pair):
        return jnp.concatenate(
            [
                coul[:, (2 * pair + t) * block : (2 * pair + t + 1) * block, :].reshape(z_cols, n_occ)
                for t in range(2)
            ],
            axis=1,
        )

    z = jnp.zeros((z_rows, z_cols), f32)
    for pair in range(pairs):
        left = jnp.concatenate(
            [
                jnp.concatenate(
                    [
                        x_t[
                            (2 * pair + t) * block : (2 * pair + t + 1) * block,
                            n * n_occ : (n + 1) * n_occ,
                        ]
                        for n in range(n_trial)
                    ],
                    axis=0,
                )
                for t in range(2)
            ],
            axis=1,
        )
        z = z + lax.dot_general(left, coul_block(pair), NT_DIMS, preferred_element_type=f32)
    same = (
        lax.broadcasted_iota(jnp.int32, (z_rows, z_cols), 0) % block
        == lax.broadcasted_iota(jnp.int32, (z_rows, z_cols), 1) % block
    )
    z = jnp.where(same, z, 0.0).reshape(n_trial, block, z_cols)
    z = jnp.broadcast_to(jnp.sum(z, axis=1, keepdims=True), (n_trial, block, z_cols))
    z = z.reshape(z_rows, z_cols)
    lanes = 128
    ones = (
        lax.broadcasted_iota(jnp.int32, (lanes, lanes), 0) // block
        == lax.broadcasted_iota(jnp.int32, (lanes, lanes), 1) // block
    ).astype(f32)
    coef = jnp.concatenate(
        [
            jnp.dot(
                z[:, c * lanes : (c + 1) * lanes],
                ones,
                precision=lax.Precision.HIGHEST,
                preferred_element_type=f32,
            )
            for c in range(z_cols // lanes)
        ],
        axis=1,
    )
    spread = jnp.where(same, coef, 0.0).astype(bf16)
    total[...] = jnp.zeros_like(total)
    for pair in range(pairs):
        part = 2.0 * jnp.dot(spread, coul_block(pair), preferred_element_type=f32)
        for t in range(2):
            for n in range(n_trial):
                total[n, (2 * pair + t) * block : (2 * pair + t + 1) * block, :] = part[
                    n * block : (n + 1) * block, t * n_occ : (t + 1) * n_occ
                ]

    for half in range(2):
        x_half = x_t[:n_virt, half * half_cols : (half + 1) * half_cols]

        def exchange(index, carry, half=half, x_half=x_half):
            first = index * group
            halfway = jnp.dot(
                vv[pl.ds(first, group)].reshape(group * n_virt, n_virt),
                x_half,
                preferred_element_type=f32,
            ).astype(bf16)
            left = jnp.concatenate(
                [
                    jnp.concatenate(
                        [
                            halfway[p * n_virt : (p + 1) * n_virt, n * n_occ : (n + 1) * n_occ]
                            for p in range(group)
                        ],
                        axis=1,
                    )
                    for n in range(half_trials)
                ],
                axis=0,
            )
            right = jnp.concatenate([oo[first + p] for p in range(group)], axis=1)
            part = lax.dot_general(left, right, NT_DIMS, preferred_element_type=f32)
            for n in range(half_trials):
                at = half * half_trials + n
                total[at, :n_virt, :] = (
                    total[at, :n_virt, :] - part[n * n_virt : (n + 1) * n_virt, :]
                )
            return carry

        lax.fori_loop(0, aux_local // group, exchange, 0)
        outgoing[half] = jnp.concatenate(
            [
                total[half * half_trials + n].T.reshape(n_dev, rows, width)
                for n in range(half_trials)
            ],
            axis=1,
        ).astype(bf16)
        each(lambda step, half=half: sum_copy(half, step).start())
        incoming[half, me] = outgoing[half, me]

    row_at = lax.broadcasted_iota(jnp.int32, (rows, n_occ), 0) + me * rows
    col_at = lax.broadcasted_iota(jnp.int32, (rows, n_occ), 1)
    occ_rows = jnp.sum(jnp.where(row_at == col_at, occ_ref[...], 0.0), axis=1, keepdims=True)
    diagonal = vir_ref[...] - occ_rows

    def whole(value):
        return jnp.sum(jnp.sum(value, axis=0, keepdims=True), axis=1, keepdims=True)

    numer, denom = [], []
    for n in range(n_trial):
        own = x_ref[n]
        square = own * own
        x_n = x_t[:, n * n_occ : (n + 1) * n_occ].astype(f32)
        numer.append(whole(x_n * total[n]) + whole(diagonal * square))
        denom.append(whole(square))
    for n in range(n_trial):
        scalars_out[n : n + 1, :] = jnp.broadcast_to(numer[n], (1, lanes))
        scalars_out[n_trial + n : n_trial + n + 1, :] = jnp.broadcast_to(denom[n], (1, lanes))
    each(lambda step: scalar_copy(step).start())
    scalars_in[me] = scalars_out[...]

    for half in range(2):
        each(lambda step, half=half: sum_copy(half, step).wait_recv())
    each(lambda step: scalar_copy(step).wait_recv())

    sums = jnp.sum(scalars_in[...], axis=0)
    precond = []
    for n in range(n_trial):
        if n % half_trials == 0:
            summed = jnp.sum(incoming[n // half_trials].astype(f32), axis=0)
        at = (n % half_trials) * rows
        own = x_ref[n]
        sigma = diagonal * own + summed[at : at + rows, :n_virt]
        sigma_ref[n] = sigma
        omega = sums[n : n + 1, :1] / (sums[n_trial + n : n_trial + n + 1, :1] + 1e-06)
        resid = sigma - omega * own
        precond.append(resid / jnp.maximum(jnp.abs(diagonal - omega), 1.0))
        norms_out[n : n + 1, :] = jnp.broadcast_to(whole(precond[n] * precond[n]), (1, lanes))
    each(lambda step: norm_copy(step).start())
    norms_in[me] = norms_out[...]
    each(lambda step: norm_copy(step).wait_recv())
    norms = jnp.sum(norms_in[...], axis=0)
    count = float(n_occ * n_virt)
    for n in range(n_trial):
        update_ref[n] = precond[n] * lax.rsqrt(norms[n : n + 1, :1] / count + 1e-06)

    each(lambda step: gather_copy(step).wait_send())
    for half in range(2):
        each(lambda step, half=half: sum_copy(half, step).wait_send())
    each(lambda step: scalar_copy(step).wait_send())
    each(lambda step: norm_copy(step).wait_send())


def on_device(n_dev, trial_vecs, occ_energy, vir_energy, coul_ov, exch_oo, exch_vv):
    n_trial, rows, n_virt = trial_vecs.shape
    aux_local, n_occ, _ = exch_oo.shape
    width = -(-n_virt // 128) * 128
    half_rows = n_trial // 2 * rows
    vmem = pl.BlockSpec(memory_space=pltpu.VMEM)
    anywhere = pl.BlockSpec(memory_space=pl.ANY)
    out = jax.ShapeDtypeStruct(trial_vecs.shape, jnp.float32)
    dma = pltpu.SemaphoreType.DMA
    return pl.pallas_call(
        functools.partial(sigma_kernel, n_dev, math.gcd(aux_local, 4)),
        out_shape=(out, out),
        in_specs=[vmem] * 3 + [anywhere] * 3,
        out_specs=(vmem, vmem),
        scratch_shapes=[
            pltpu.VMEM((aux_local, n_virt, n_occ), jnp.bfloat16),
            pltpu.VMEM((aux_local, n_occ, n_occ), jnp.bfloat16),
            pltpu.VMEM((aux_local, n_virt, n_virt), jnp.bfloat16),
            pltpu.VMEM((n_trial * rows, width), jnp.float32),
            pltpu.VMEM((n_dev, n_trial * rows, width), jnp.bfloat16),
            pltpu.VMEM((width, n_trial * n_occ), jnp.bfloat16),
            pltpu.VMEM((n_trial, width, n_occ), jnp.float32),
            pltpu.VMEM((2, n_dev, half_rows, width), jnp.bfloat16),
            pltpu.VMEM((2, n_dev, half_rows, width), jnp.bfloat16),
            pltpu.VMEM((2 * n_trial, 128), jnp.float32),
            pltpu.VMEM((n_dev, 2 * n_trial, 128), jnp.float32),
            pltpu.VMEM((2 * n_trial, 128), jnp.float32),
            pltpu.VMEM((n_dev, 2 * n_trial, 128), jnp.float32),
            dma((3,)),
            dma((n_dev,)),
            dma((n_dev,)),
            dma((2, n_dev)),
            dma((2, n_dev)),
            dma((n_dev,)),
            dma((n_dev,)),
            dma((n_dev,)),
            dma((n_dev,)),
        ],
        compiler_params=pltpu.CompilerParams(
            collective_id=0, has_side_effects=True, vmem_limit_bytes=56 * 1024 * 1024
        ),
    )(
        trial_vecs,
        occ_energy[None, :],
        vir_energy[None, :],
        coul_ov.transpose(0, 2, 1),
        exch_oo,
        exch_vv,
    )


def contract(rows_x, coul_ov, exch_oo, exch_vv):
    aux_coef = jnp.einsum("pia,nia->np", coul_ov, rows_x, preferred_element_type=jnp.float32)
    coulomb = jnp.einsum(
        "pia,np->nia", coul_ov, aux_coef.astype(jnp.bfloat16), preferred_element_type=jnp.float32
    )
    aux_local, n_occ, _ = exch_oo.shape
    n_virt = exch_vv.shape[1]
    group_size = math.gcd(aux_local, 16)
    vv_groups = exch_vv.reshape(aux_local // group_size, group_size, n_virt, n_virt)
    oo_groups = exch_oo.reshape(aux_local // group_size, group_size, n_occ, n_occ)

    def advance(running, parts_pair):
        vv_part, oo_part = parts_pair
        halfway = jnp.einsum(
            "pab,njb->pnja", vv_part, rows_x, preferred_element_type=jnp.float32
        ).astype(jnp.bfloat16)
        return (
            running
            + jnp.einsum("pij,pnja->nia", oo_part, halfway, preferred_element_type=jnp.float32),
            None,
        )

    exchange, _ = lax.scan(advance, jnp.zeros(rows_x.shape, jnp.float32), (vv_groups, oo_groups))
    return 2.0 * coulomb - exchange


def on_device_plain(trial_vecs, occ_energy, vir_energy, coul_ov, exch_oo, exch_vv):
    local_rows = trial_vecs.shape[1]
    n_occ, n_virt = coul_ov.shape[1:]
    row_start = lax.axis_index("aux") * local_rows
    rows_x = lax.all_gather(trial_vecs.astype(jnp.bfloat16), "aux", axis=1, tiled=True)
    summed = lax.psum_scatter(
        contract(rows_x, coul_ov, exch_oo, exch_vv), "aux", scatter_dimension=1, tiled=True
    )
    occ_rows = lax.dynamic_slice_in_dim(occ_energy, row_start, local_rows, 0)
    diagonal = vir_energy[None, :] - occ_rows[:, None]
    sigma = diagonal[None] * trial_vecs + summed
    sums = lax.psum(
        jnp.stack([jnp.sum(trial_vecs * sigma, (1, 2)), jnp.sum(trial_vecs * trial_vecs, (1, 2))]),
        "aux",
    )
    omega = (sums[0] / (sums[1] + 1e-06))[:, None, None]
    precond = (sigma - omega * trial_vecs) / jnp.maximum(jnp.abs(diagonal[None] - omega), 1.0)
    squares = lax.psum(jnp.sum(precond * precond, axis=(1, 2)), "aux") / (n_occ * n_virt)
    return sigma, precond * lax.rsqrt(squares + 1e-06)[:, None, None]


def solution(mesh):
    n_dev = mesh.shape["aux"]

    def body(trial_vecs, occ_energy, vir_energy, coul_ov, exch_oo, exch_vv):
        n_trial, rows, n_virt = trial_vecs.shape
        aux_local, n_occ, _ = exch_oo.shape
        tiled = (
            n_trial % 4 == 0
            and rows % 8 == 0
            and n_occ % 128 == 0
            and n_virt % 32 == 0
            and aux_local % 8 == 0
        )
        args = (trial_vecs, occ_energy, vir_energy, coul_ov, exch_oo, exch_vv)
        return on_device(n_dev, *args) if tiled else on_device_plain(*args)

    in_specs = (
        P("geom", "aux", None),
        P("geom"),
        P("geom"),
        P(("geom", "aux"), None, None),
        P(("geom", "aux"), None, None),
        P(("geom", "aux"), None, None),
    )
    out_specs = (P("geom", "aux", None), P("geom", "aux", None))
    return jax.shard_map(body, mesh=mesh, in_specs=in_specs, out_specs=out_specs, check_vma=False)
```

time: 160 us -> 51.4 us (0.32)
  waiting for transfers between devices: 87 us -> 0 us
  Pallas kernels: 0 us -> 47.7 us
  blocking collectives: 24.6 us -> 0 us
  matrix products: 21.2 us -> 0 us
  between operations: 14.1 us -> 0.64 us
  local copies, waits for them, and re-layouts: 9.57 us -> 2.75 us
  other arithmetic: 3.17 us -> 0 us
    psum x1 -> x0, waiting for transfers between devices: 86.9 us -> none  [on_device(): summed = lax.psum(2.0 * coulomb - exchange, 'aux')]
    pallas_call x0 -> x1, Pallas kernels: none -> 47.7 us  [on_device(): pl.pallas_call(functools.partial(sigma_kernel, n_dev, math.gcd(aux_local,...]
    all_gather x1 -> x0, blocking collectives: 24.6 us -> none  [on_device(): wide_x = lax.all_gather(trial_vecs, 'aux', axis=1, tiled=True)]
    dot_general x5 -> x0, matrix products: 21.2 us -> none  [the longest x4 15.1 us: advance(): jnp.einsum('pij,pnja->nia', oo_part, halfway, preferred_element_type=jnp....]
    unnamed x9 -> x2, local copies, waits for them, and re-layouts: 9.34 us -> 2.75 us
    reduce_sum x3 -> x0, other arithmetic: 1.9 us -> none  [the longest x1 1.21 us: on_device(): jnp.sum(wide_x * sigma_all, axis=(1, 2))]
  transfers between devices with their start and end apart: 1 -> 0, of which waited for: 1 -> 0; matrix products, arithmetic and copies ran while one was open for 0% -> 0% of each run, Pallas kernels for 0% -> 0%
where the time goes in v1:
time: 51.4 us; the launch traced here: 51.1 us
  Pallas kernels  47.7 us (93%)
  local copies, waits for them, and re-layouts  2.75 us (5%)
  between operations  0.64 us (1%)
    pallas_call x1, Pallas kernels, on_device(): pl.pallas_call(functools.partial(sigma_kernel, n_dev, math.gcd(aux_local,...  47.7 us
    unnamed x2, local copies, waits for them, and re-layouts  2.75 us

profile of v1, /device:TPU:0, one launch (start us, length us, event | category | flops | bytes accessed | tf_op | source)
XLA Modules:
  0.0 51.1 jit_solution(16154438839683115748)
XLA Ops:
  0.6 47.7 %shard_map.77 = (f32[4,8,224]{2,1,0:T(8,128)}, f32[4,8,224]{2,1,0:T(8,128)}) custom-call(f32[4,8,224]{2,1,0:T(8,128)} %x_ref.1, f32[1,128]{1,0:T(1,128)} %bitcast.5, f32[1,224]{1,0:T(1,128)} %bitcast.4, bf16[64,224,128]{2,1,0:T(8,128)(2,1)} %bitcast.3, bf16[64,128,128]{2,1,0:T(8,128)(2,1)} %oo_hbm.1, bf16[64,224,224]{2,1,0:T(8,128)(2,1)} %vv_hbm.1), custom_call_target="tpu_custom_call" | custom-call | tf_op jit(solution)/shard_map/pallas_call | solution.py:293
  48.3 1.4 %copy.10 = f32[4,8,224]{2,1,0:T(8,128)} copy(f32[4,8,224]{2,1,0:T(8,128)} %get-tuple-element.4) | data formatting | bytes 57344
  49.7 1.4 %copy.11 = f32[4,8,224]{2,1,0:T(8,128)} copy(f32[4,8,224]{2,1,0:T(8,128)} %get-tuple-element.5) | data formatting | bytes 57344

commit v2 on v1

--- a/solution.py
+++ b/solution.py
@@ -36,6 +36,8 @@
     scalars_in,
     norms_out,
     norms_in,
+    halfway_a,
+    halfway_b,
     load_sem,
     gather_send,
     gather_recv,
@@ -155,26 +157,23 @@
         lax.broadcasted_iota(jnp.int32, (z_rows, z_cols), 0) % block
         == lax.broadcasted_iota(jnp.int32, (z_rows, z_cols), 1) % block
     )
-    z = jnp.where(same, z, 0.0).reshape(n_trial, block, z_cols)
-    z = jnp.broadcast_to(jnp.sum(z, axis=1, keepdims=True), (n_trial, block, z_cols))
-    z = z.reshape(z_rows, z_cols)
+    z = jnp.sum(jnp.where(same, z, 0.0).reshape(n_trial, block, z_cols), axis=1)
     lanes = 128
+    chunks = z_cols // lanes
     ones = (
         lax.broadcasted_iota(jnp.int32, (lanes, lanes), 0) // block
         == lax.broadcasted_iota(jnp.int32, (lanes, lanes), 1) // block
-    ).astype(f32)
+    ).astype(bf16)
+    z = jnp.concatenate([z[:, c * lanes : (c + 1) * lanes] for c in range(chunks)], axis=0)
+    coef = jnp.zeros_like(z)
+    for _ in range(3):
+        piece = z.astype(bf16)
+        z = z - piece.astype(f32)
+        coef = coef + jnp.dot(piece, ones, preferred_element_type=f32)
     coef = jnp.concatenate(
-        [
-            jnp.dot(
-                z[:, c * lanes : (c + 1) * lanes],
-                ones,
-                precision=lax.Precision.HIGHEST,
-                preferred_element_type=f32,
-            )
-            for c in range(z_cols // lanes)
-        ],
-        axis=1,
-    )
+        [coef[c * n_trial : (c + 1) * n_trial] for c in range(chunks)], axis=1
+    )
+    coef = jnp.broadcast_to(coef[:, None, :], (n_trial, block, z_cols)).reshape(z_rows, z_cols)
     spread = jnp.where(same, coef, 0.0).astype(bf16)
     total[...] = jnp.zeros_like(total)
     for pair in range(pairs):
@@ -188,18 +187,19 @@
     for half in range(2):
         x_half = x_t[:n_virt, half * half_cols : (half + 1) * half_cols]
 
-        def exchange(index, carry, half=half, x_half=x_half):
-            first = index * group
-            halfway = jnp.dot(
-                vv[pl.ds(first, group)].reshape(group * n_virt, n_virt),
+        def first_step(index, slot, x_half=x_half):
+            slot[...] = jnp.dot(
+                vv[pl.ds(index * group, group)].reshape(group * n_virt, n_virt),
                 x_half,
                 preferred_element_type=f32,
             ).astype(bf16)
+
+        def second_step(index, slot, half=half):
             left = jnp.concatenate(
                 [
                     jnp.concatenate(
                         [
-                            halfway[p * n_virt : (p + 1) * n_virt, n * n_occ : (n + 1) * n_occ]
+                            slot[p * n_virt : (p + 1) * n_virt, n * n_occ : (n + 1) * n_occ]
                             for p in range(group)
                         ],
                         axis=1,
@@ -208,16 +208,27 @@
                 ],
                 axis=0,
             )
-            right = jnp.concatenate([oo[first + p] for p in range(group)], axis=1)
+            right = jnp.concatenate([oo[index * group + p] for p in range(group)], axis=1)
             part = lax.dot_general(left, right, NT_DIMS, preferred_element_type=f32)
             for n in range(half_trials):
                 at = half * half_trials + n
                 total[at, :n_virt, :] = (
                     total[at, :n_virt, :] - part[n * n_virt : (n + 1) * n_virt, :]
                 )
+
+        def exchange(index, carry):
+            first_step(2 * index + 1, halfway_b)
+            second_step(2 * index, halfway_a)
+            first_step(2 * index + 2, halfway_a)
+            second_step(2 * index + 1, halfway_b)
             return carry
 
-        lax.fori_loop(0, aux_local // group, exchange, 0)
+        groups = aux_local // group
+        first_step(0, halfway_a)
+        lax.fori_loop(0, groups // 2 - 1, exchange, 0)
+        first_step(groups - 1, halfway_b)
+        second_step(groups - 2, halfway_a)
+        second_step(groups - 1, halfway_b)
         outgoing[half] = jnp.concatenate(
             [
                 total[half * half_trials + n].T.reshape(n_dev, rows, width)
@@ -286,12 +297,13 @@
     aux_local, n_occ, _ = exch_oo.shape
     width = -(-n_virt // 128) * 128
     half_rows = n_trial // 2 * rows
+    group = math.gcd(aux_local // 2, 8)
     vmem = pl.BlockSpec(memory_space=pltpu.VMEM)
     anywhere = pl.BlockSpec(memory_space=pl.ANY)
     out = jax.ShapeDtypeStruct(trial_vecs.shape, jnp.float32)
     dma = pltpu.SemaphoreType.DMA
     return pl.pallas_call(
-        functools.partial(sigma_kernel, n_dev, math.gcd(aux_local, 4)),
+        functools.partial(sigma_kernel, n_dev, group),
         out_shape=(out, out),
         in_specs=[vmem] * 3 + [anywhere] * 3,
         out_specs=(vmem, vmem),
@@ -309,6 +321,8 @@
             pltpu.VMEM((n_dev, 2 * n_trial, 128), jnp.float32),
             pltpu.VMEM((2 * n_trial, 128), jnp.float32),
             pltpu.VMEM((n_dev, 2 * n_trial, 128), jnp.float32),
+            pltpu.VMEM((group * n_virt, n_trial // 2 * n_occ), jnp.bfloat16),
+            pltpu.VMEM((group * n_virt, n_trial // 2 * n_occ), jnp.bfloat16),
             dma((3,)),
             dma((n_dev,)),
             dma((n_dev,)),
@@ -390,7 +404,7 @@
             and rows % 8 == 0
             and n_occ % 128 == 0
             and n_virt % 32 == 0
-            and aux_local % 8 == 0
+            and aux_local % 16 == 0
         )
         args = (trial_vecs, occ_energy, vir_energy, coul_ov, exch_oo, exch_vv)
         return on_device(n_dev, *args) if tiled else on_device_plain(*args)

time: 51.4 us -> 42.8 us (0.83)
  Pallas kernels: 47.7 us -> 39.1 us
    pallas_call x1, Pallas kernels: 47.7 us -> 39.1 us  [on_device(): pl.pallas_call(functools.partial(sigma_kernel, n_dev, group), out_shape=(...]
where the time goes in v2:
time: 42.8 us; the launch traced here: 42.5 us
  Pallas kernels  39.1 us (91%)
  local copies, waits for them, and re-layouts  2.75 us (6%)
  between operations  0.64 us (1%)
    pallas_call x1, Pallas kernels, on_device(): pl.pallas_call(functools.partial(sigma_kernel, n_dev, group), out_shape=(...  39.1 us
    unnamed x2, local copies, waits for them, and re-layouts  2.75 us

profile of v2, /device:TPU:0, one launch (start us, length us, event | category | flops | bytes accessed | tf_op | source)
XLA Modules:
  0.0 42.5 jit_solution(10794611069532636062)
XLA Ops:
  0.6 39.1 %shard_map.77 = (f32[4,8,224]{2,1,0:T(8,128)}, f32[4,8,224]{2,1,0:T(8,128)}) custom-call(f32[4,8,224]{2,1,0:T(8,128)} %x_ref.1, f32[1,128]{1,0:T(1,128)} %bitcast.5, f32[1,224]{1,0:T(1,128)} %bitcast.4, bf16[64,224,128]{2,1,0:T(8,128)(2,1)} %bitcast.3, bf16[64,128,128]{2,1,0:T(8,128)(2,1)} %oo_hbm.1, bf16[64,224,224]{2,1,0:T(8,128)(2,1)} %vv_hbm.1), custom_call_target="tpu_custom_call" | custom-call | tf_op jit(solution)/shard_map/pallas_call | solution.py:305
  39.7 1.4 %copy.10 = f32[4,8,224]{2,1,0:T(8,128)} copy(f32[4,8,224]{2,1,0:T(8,128)} %get-tuple-element.4) | data formatting | bytes 57344
  41.1 1.4 %copy.11 = f32[4,8,224]{2,1,0:T(8,128)} copy(f32[4,8,224]{2,1,0:T(8,128)} %get-tuple-element.5) | data formatting | bytes 57344

commit v3 on v2

--- a/solution.py
+++ b/solution.py
@@ -88,8 +88,24 @@
             device_id_type=MESH,
         )
 
-    def gather_copy(step):
-        return to_peer(gathered.at[me], gathered.at[me], gather_send, gather_recv, step)
+    pair = me + 1 - 2 * lax.rem(me, 2)
+    chip_steps = sorted(range(2, n_dev, 2), key=lambda step: -min(step, n_dev - step))
+
+    def block_copy(owner, peer, sem_at):
+        return pltpu.make_async_remote_copy(
+            src_ref=gathered.at[owner],
+            dst_ref=gathered.at[owner],
+            send_sem=gather_send.at[sem_at],
+            recv_sem=gather_recv.at[sem_at],
+            device_id={"aux": peer},
+            device_id_type=MESH,
+        )
+
+    def direct_copy(step):
+        return block_copy(me, lax.rem(me + step, n_dev), step)
+
+    def passed_copy(step):
+        return block_copy(lax.rem(me + n_dev - step, n_dev), pair, step + 1)
 
     def sum_copy(half, step):
         peer = lax.rem(me + step, n_dev)
@@ -110,10 +126,17 @@
 
         lax.fori_loop(1, n_dev, body, 0)
 
-    each(lambda step: gather_copy(step).start())
+    for step in chip_steps:
+        direct_copy(step).start()
+    block_copy(me, pair, 1).start()
     for load in loads:
         load.wait()
-    each(lambda step: gather_copy(step).wait_recv())
+    for step in reversed(chip_steps):
+        direct_copy(step).wait_recv()
+        passed_copy(step).start()
+    block_copy(me, pair, 1).wait_recv()
+    for step in reversed(chip_steps):
+        passed_copy(step).wait_recv()
 
     wide = gathered[...].astype(f32).reshape(n_dev, n_trial, rows, width)
     for n in range(n_trial):
@@ -285,11 +308,19 @@
     for n in range(n_trial):
         update_ref[n] = precond[n] * lax.rsqrt(norms[n : n + 1, :1] / count + 1e-06)
 
-    each(lambda step: gather_copy(step).wait_send())
+    block_copy(me, pair, 1).wait_send()
+    for step in chip_steps:
+        direct_copy(step).wait_send()
+        passed_copy(step).wait_send()
     for half in range(2):
         each(lambda step, half=half: sum_copy(half, step).wait_send())
     each(lambda step: scalar_copy(step).wait_send())
     each(lambda step: norm_copy(step).wait_send())
+
+
+def hand_over(sigma_in, update_in, sigma_ref, update_ref):
+    sigma_ref[...] = sigma_in[...]
+    update_ref[...] = update_in[...]
 
 
 def on_device(n_dev, trial_vecs, occ_energy, vir_energy, coul_ov, exch_oo, exch_vv):
@@ -302,7 +333,7 @@
     anywhere = pl.BlockSpec(memory_space=pl.ANY)
     out = jax.ShapeDtypeStruct(trial_vecs.shape, jnp.float32)
     dma = pltpu.SemaphoreType.DMA
-    return pl.pallas_call(
+    sigma, update = pl.pallas_call(
         functools.partial(sigma_kernel, n_dev, group),
         out_shape=(out, out),
         in_specs=[vmem] * 3 + [anywhere] * 3,
@@ -344,6 +375,9 @@
         exch_oo,
         exch_vv,
     )
+    return pl.pallas_call(
+        hand_over, out_shape=(out, out), in_specs=[vmem] * 2, out_specs=(vmem, vmem)
+    )(sigma, update)
 
 
 def contract(rows_x, coul_ov, exch_oo, exch_vv):
@@ -405,6 +439,7 @@
             and n_occ % 128 == 0
             and n_virt % 32 == 0
             and aux_local % 16 == 0
+            and n_dev % 2 == 0
         )
         args = (trial_vecs, occ_energy, vir_energy, coul_ov, exch_oo, exch_vv)
         return on_device(n_dev, *args) if tiled else on_device_plain(*args)

time: 42.8 us -> 40.1 us (0.937)
  local copies, waits for them, and re-layouts: 2.75 us -> 0 us
    unnamed x2 -> x0, local copies, waits for them, and re-layouts: 2.75 us -> none
    pallas_call x0 -> x1, Pallas kernels: none -> 1.4 us  [on_device(): pl.pallas_call(hand_over, out_shape=(out, out), in_specs=[vmem] * 2, out_...]
    pallas_call x1, Pallas kernels: 39.1 us -> 37.8 us  [on_device(): pl.pallas_call(functools.partial(sigma_kernel, n_dev, group), out_shape=(...]
where the time goes in v3:
time: 40.1 us; the launch traced here: 39.8 us
  Pallas kernels  39.2 us (98%)
  between operations  0.64 us (2%)
    pallas_call x1, Pallas kernels, on_device(): pl.pallas_call(functools.partial(sigma_kernel, n_dev, group), out_shape=(...  37.8 us
    pallas_call x1, Pallas kernels, on_device(): pl.pallas_call(hand_over, out_shape=(out, out), in_specs=[vmem] * 2, out_...  1.4 us

profile of v3, /device:TPU:0, one launch (start us, length us, event | category | flops | bytes accessed | tf_op | source)
XLA Modules:
  0.0 39.8 jit_solution(10711574580268511755)
XLA Ops:
  0.6 37.8 %shard_map.77 = (f32[4,8,224]{2,1,0:T(8,128)}, f32[4,8,224]{2,1,0:T(8,128)}) custom-call(f32[4,8,224]{2,1,0:T(8,128)} %x_ref.1, f32[1,128]{1,0:T(1,128)} %bitcast.5, f32[1,224]{1,0:T(1,128)} %bitcast.4, bf16[64,224,128]{2,1,0:T(8,128)(2,1)} %bitcast.3, bf16[64,128,128]{2,1,0:T(8,128)(2,1)} %oo_hbm.1, bf16[64,224,224]{2,1,0:T(8,128)(2,1)} %vv_hbm.1), custom_call_target="tpu_custom_call" | custom-call | tf_op jit(solution)/shard_map/pallas_call | solution.py:336
  38.4 1.4 %shard_map.78 = (f32[4,8,224]{2,1,0:T(8,128)}, f32[4,8,224]{2,1,0:T(8,128)}) custom-call(f32[4,8,224]{2,1,0:T(8,128)} %get-tuple-element.4.sigma_in, f32[4,8,224]{2,1,0:T(8,128)} %get-tuple-element.5.update_in), custom_call_target="tpu_custom_call" | custom-call | tf_op jit(solution)/shard_map/pallas_call | solution.py:378

commit v4 on v3

--- a/solution.py
+++ b/solution.py
@@ -9,7 +9,6 @@
 from jax.sharding import PartitionSpec as P
 
 MESH = pl.DeviceIdType.MESH
-NT_DIMS = (((1,), (1,)), ((), ()))
 
 
 def sigma_kernel(
@@ -38,6 +37,8 @@
     norms_in,
     halfway_a,
     halfway_b,
+    coul_t,
+    oo_t,
     load_sem,
     gather_send,
     gather_recv,
@@ -58,7 +59,7 @@
 
     loads = [
         pltpu.make_async_copy(source, target, load_sem.at[slot])
-        for slot, (source, target) in enumerate(((coul_hbm, coul), (vv_hbm, vv), (oo_hbm, oo)))
+        for slot, (source, target) in enumerate(((coul_hbm, coul), (oo_hbm, oo), (vv_hbm, vv)))
     ]
     for load in loads:
         load.start()
@@ -129,8 +130,25 @@
     for step in chip_steps:
         direct_copy(step).start()
     block_copy(me, pair, 1).start()
-    for load in loads:
-        load.wait()
+
+    block = 16
+    tiles = n_virt // block
+    z_rows, z_cols = n_trial * block, aux_local * block
+    loads[0].wait()
+    for t in range(tiles):
+        coul_t[t * n_occ : (t + 1) * n_occ, :] = (
+            coul[:, t * block : (t + 1) * block, :].reshape(z_cols, n_occ).T
+        )
+    loads[1].wait()
+
+    def turn(index, carry):
+        for p in range(group):
+            at = index * group + p
+            oo_t[pl.ds(at * n_occ, n_occ), :] = oo[at].T
+        return carry
+
+    lax.fori_loop(0, aux_local // group, turn, 0)
+    loads[2].wait()
     for step in reversed(chip_steps):
         direct_copy(step).wait_recv()
         passed_copy(step).start()
@@ -144,38 +162,29 @@
             wide[:, n].reshape(n_occ, width).T.astype(bf16)
         )
 
-    block = 16
-    pairs = n_virt // (2 * block)
-    z_rows, z_cols = n_trial * block, aux_local * block
-
-    def coul_block(pair):
-        return jnp.concatenate(
-            [
-                coul[:, (2 * pair + t) * block : (2 * pair + t + 1) * block, :].reshape(z_cols, n_occ)
-                for t in range(2)
-            ],
-            axis=1,
-        )
-
-    z = jnp.zeros((z_rows, z_cols), f32)
-    for pair in range(pairs):
-        left = jnp.concatenate(
-            [
-                jnp.concatenate(
-                    [
-                        x_t[
-                            (2 * pair + t) * block : (2 * pair + t + 1) * block,
-                            n * n_occ : (n + 1) * n_occ,
-                        ]
-                        for n in range(n_trial)
-                    ],
-                    axis=0,
-                )
-                for t in range(2)
-            ],
-            axis=1,
-        )
-        z = z + lax.dot_general(left, coul_block(pair), NT_DIMS, preferred_element_type=f32)
+    def first_step(half, index, slot):
+        slot[...] = jnp.dot(
+            vv[pl.ds(index * group, group)].reshape(group * n_virt, n_virt),
+            x_t[:n_virt, half * half_cols : (half + 1) * half_cols],
+            preferred_element_type=f32,
+        ).astype(bf16)
+
+    first_step(0, 0, halfway_a)
+
+    left = jnp.concatenate(
+        [
+            jnp.concatenate(
+                [
+                    x_t[t * block : (t + 1) * block, n * n_occ : (n + 1) * n_occ]
+                    for n in range(n_trial)
+                ],
+                axis=0,
+            )
+            for t in range(tiles)
+        ],
+        axis=1,
+    )
+    z = jnp.dot(left, coul_t[...], preferred_element_type=f32)
     same = (
         lax.broadcasted_iota(jnp.int32, (z_rows, z_cols), 0) % block
         == lax.broadcasted_iota(jnp.int32, (z_rows, z_cols), 1) % block
@@ -199,8 +208,15 @@
     coef = jnp.broadcast_to(coef[:, None, :], (n_trial, block, z_cols)).reshape(z_rows, z_cols)
     spread = jnp.where(same, coef, 0.0).astype(bf16)
     total[...] = jnp.zeros_like(total)
-    for pair in range(pairs):
-        part = 2.0 * jnp.dot(spread, coul_block(pair), preferred_element_type=f32)
+    for pair in range(tiles // 2):
+        right = jnp.concatenate(
+            [
+                coul[:, (2 * pair + t) * block : (2 * pair + t + 1) * block, :].reshape(z_cols, n_occ)
+                for t in range(2)
+            ],
+            axis=1,
+        )
+        part = 2.0 * jnp.dot(spread, right, preferred_element_type=f32)
         for t in range(2):
             for n in range(n_trial):
                 total[n, (2 * pair + t) * block : (2 * pair + t + 1) * block, :] = part[
@@ -208,15 +224,6 @@
                 ]
 
     for half in range(2):
-        x_half = x_t[:n_virt, half * half_cols : (half + 1) * half_cols]
-
-        def first_step(index, slot, x_half=x_half):
-            slot[...] = jnp.dot(
-                vv[pl.ds(index * group, group)].reshape(group * n_virt, n_virt),
-                x_half,
-                preferred_element_type=f32,
-            ).astype(bf16)
-
         def second_step(index, slot, half=half):
             left = jnp.concatenate(
                 [
@@ -231,26 +238,27 @@
                 ],
                 axis=0,
             )
-            right = jnp.concatenate([oo[index * group + p] for p in range(group)], axis=1)
-            part = lax.dot_general(left, right, NT_DIMS, preferred_element_type=f32)
+            right = oo_t[pl.ds(index * (group * n_occ), group * n_occ), :]
+            part = jnp.dot(left, right, preferred_element_type=f32)
             for n in range(half_trials):
                 at = half * half_trials + n
                 total[at, :n_virt, :] = (
                     total[at, :n_virt, :] - part[n * n_virt : (n + 1) * n_virt, :]
                 )
 
-        def exchange(index, carry):
-            first_step(2 * index + 1, halfway_b)
+        def exchange(index, carry, half=half):
+            first_step(half, 2 * index + 1, halfway_b)
             second_step(2 * index, halfway_a)
-            first_step(2 * index + 2, halfway_a)
+            first_step(half, 2 * index + 2, halfway_a)
             second_step(2 * index + 1, halfway_b)
             return carry
 
         groups = aux_local // group
-        first_step(0, halfway_a)
         lax.fori_loop(0, groups // 2 - 1, exchange, 0)
-        first_step(groups - 1, halfway_b)
+        first_step(half, groups - 1, halfway_b)
         second_step(groups - 2, halfway_a)
+        if half == 0:
+            first_step(1, 0, halfway_a)
         second_step(groups - 1, halfway_b)
         outgoing[half] = jnp.concatenate(
             [
@@ -354,6 +362,8 @@
             pltpu.VMEM((n_dev, 2 * n_trial, 128), jnp.float32),
             pltpu.VMEM((group * n_virt, n_trial // 2 * n_occ), jnp.bfloat16),
             pltpu.VMEM((group * n_virt, n_trial // 2 * n_occ), jnp.bfloat16),
+            pltpu.VMEM((n_virt * n_occ // 16, aux_local * 16), jnp.bfloat16),
+            pltpu.VMEM((aux_local * n_occ, n_occ), jnp.bfloat16),
             dma((3,)),
             dma((n_dev,)),
             dma((n_dev,)),

time: 40.1 us -> 39.1 us (0.975)
  Pallas kernels: 39.2 us -> 38.2 us
    pallas_call x1, Pallas kernels: 37.8 us -> 36.8 us  [on_device(): pl.pallas_call(functools.partial(sigma_kernel, n_dev, group), out_shape=(...]
where the time goes in v4:
time: 39.1 us; the launch traced here: 38.9 us
  Pallas kernels  38.2 us (98%)
  between operations  0.64 us (2%)
    pallas_call x1, Pallas kernels, on_device(): pl.pallas_call(functools.partial(sigma_kernel, n_dev, group), out_shape=(...  36.8 us
    pallas_call x1, Pallas kernels, on_device(): pl.pallas_call(hand_over, out_shape=(out, out), in_specs=[vmem] * 2, out_...  1.4 us

profile of v4, /device:TPU:0, one launch (start us, length us, event | category | flops | bytes accessed | tf_op | source)
XLA Modules:
  0.0 38.9 jit_solution(9881583151342821701)
XLA Ops:
  0.6 36.8 %shard_map.77 = (f32[4,8,224]{2,1,0:T(8,128)}, f32[4,8,224]{2,1,0:T(8,128)}) custom-call(f32[4,8,224]{2,1,0:T(8,128)} %x_ref.1, f32[1,128]{1,0:T(1,128)} %bitcast.5, f32[1,224]{1,0:T(1,128)} %bitcast.4, bf16[64,224,128]{2,1,0:T(8,128)(2,1)} %bitcast.3, bf16[64,128,128]{2,1,0:T(8,128)(2,1)} %oo_hbm.1, bf16[64,224,224]{2,1,0:T(8,128)(2,1)} %vv_hbm.1), custom_call_target="tpu_custom_call" | custom-call | tf_op jit(solution)/shard_map/pallas_call | solution.py:344
  37.5 1.4 %shard_map.78 = (f32[4,8,224]{2,1,0:T(8,128)}, f32[4,8,224]{2,1,0:T(8,128)}) custom-call(f32[4,8,224]{2,1,0:T(8,128)} %get-tuple-element.4.sigma_in, f32[4,8,224]{2,1,0:T(8,128)} %get-tuple-element.5.update_in), custom_call_target="tpu_custom_call" | custom-call | tf_op jit(solution)/shard_map/pallas_call | solution.py:388

commit v5 on v4

--- a/solution.py
+++ b/solution.py
@@ -139,6 +139,14 @@
         coul_t[t * n_occ : (t + 1) * n_occ, :] = (
             coul[:, t * block : (t + 1) * block, :].reshape(z_cols, n_occ).T
         )
+
+    def pass_on(steps):
+        for step in steps:
+            direct_copy(step).wait_recv()
+            passed_copy(step).start()
+
+    near_first = chip_steps[::-1]
+    pass_on(near_first[: len(near_first) // 2])
     loads[1].wait()
 
     def turn(index, carry):
@@ -148,10 +156,8 @@
         return carry
 
     lax.fori_loop(0, aux_local // group, turn, 0)
+    pass_on(near_first[len(near_first) // 2 :])
     loads[2].wait()
-    for step in reversed(chip_steps):
-        direct_copy(step).wait_recv()
-        passed_copy(step).start()
     block_copy(me, pair, 1).wait_recv()
     for step in reversed(chip_steps):
         passed_copy(step).wait_recv()
@@ -291,18 +297,18 @@
     each(lambda step: scalar_copy(step).start())
     scalars_in[me] = scalars_out[...]
 
+    summed = []
     for half in range(2):
         each(lambda step, half=half: sum_copy(half, step).wait_recv())
+        summed.append(jnp.sum(incoming[half].astype(f32), axis=0))
     each(lambda step: scalar_copy(step).wait_recv())
 
     sums = jnp.sum(scalars_in[...], axis=0)
     precond = []
     for n in range(n_trial):
-        if n % half_trials == 0:
-            summed = jnp.sum(incoming[n // half_trials].astype(f32), axis=0)
         at = (n % half_trials) * rows
         own = x_ref[n]
-        sigma = diagonal * own + summed[at : at + rows, :n_virt]
+        sigma = diagonal * own + summed[n // half_trials][at : at + rows, :n_virt]
         sigma_ref[n] = sigma
         omega = sums[n : n + 1, :1] / (sums[n_trial + n : n_trial + n + 1, :1] + 1e-06)
         resid = sigma - omega * own

time: 39.1 us -> 40.1 us (1.026)
  Pallas kernels: 38.2 us -> 39.2 us
    pallas_call x1, Pallas kernels: 36.8 us -> 37.8 us  [on_device(): pl.pallas_call(functools.partial(sigma_kernel, n_dev, group), out_shape=(...]
where the time goes in v5:
time: 40.1 us; the launch traced here: 39.8 us
  Pallas kernels  39.2 us (98%)
  between operations  0.64 us (2%)
    pallas_call x1, Pallas kernels, on_device(): pl.pallas_call(functools.partial(sigma_kernel, n_dev, group), out_shape=(...  37.8 us
    pallas_call x1, Pallas kernels, on_device(): pl.pallas_call(hand_over, out_shape=(out, out), in_specs=[vmem] * 2, out_...  1.4 us

profile of v5, /device:TPU:0, one launch (start us, length us, event | category | flops | bytes accessed | tf_op | source)
XLA Modules:
  0.0 39.8 jit_solution(974211740682920084)
XLA Ops:
  0.6 37.8 %shard_map.77 = (f32[4,8,224]{2,1,0:T(8,128)}, f32[4,8,224]{2,1,0:T(8,128)}) custom-call(f32[4,8,224]{2,1,0:T(8,128)} %x_ref.1, f32[1,128]{1,0:T(1,128)} %bitcast.5, f32[1,224]{1,0:T(1,128)} %bitcast.4, bf16[64,224,128]{2,1,0:T(8,128)(2,1)} %bitcast.3, bf16[64,128,128]{2,1,0:T(8,128)(2,1)} %oo_hbm.1, bf16[64,224,224]{2,1,0:T(8,128)(2,1)} %vv_hbm.1), custom_call_target="tpu_custom_call" | custom-call | tf_op jit(solution)/shard_map/pallas_call | solution.py:350
  38.4 1.4 %shard_map.78 = (f32[4,8,224]{2,1,0:T(8,128)}, f32[4,8,224]{2,1,0:T(8,128)}) custom-call(f32[4,8,224]{2,1,0:T(8,128)} %get-tuple-element.4.sigma_in, f32[4,8,224]{2,1,0:T(8,128)} %get-tuple-element.5.update_in), custom_call_target="tpu_custom_call" | custom-call | tf_op jit(solution)/shard_map/pallas_call | solution.py:394

commit v6 on v4

--- a/solution.py
+++ b/solution.py
@@ -55,11 +55,12 @@
     width = x_pad.shape[1]
     half_trials = n_trial // 2
     half_cols = half_trials * n_occ
+    lanes = 128
     f32, bf16 = jnp.float32, jnp.bfloat16
 
     loads = [
         pltpu.make_async_copy(source, target, load_sem.at[slot])
-        for slot, (source, target) in enumerate(((coul_hbm, coul), (oo_hbm, oo), (vv_hbm, vv)))
+        for slot, (source, target) in enumerate(((oo_hbm, oo), (coul_hbm, coul), (vv_hbm, vv)))
     ]
     for load in loads:
         load.start()
@@ -76,7 +77,9 @@
 
     x_pad[...] = jnp.zeros_like(x_pad)
     x_pad[:, :n_virt] = x_ref[...].reshape(n_trial * rows, n_virt)
-    gathered[me] = x_pad[...].astype(bf16)
+    half_rows = half_trials * rows
+    for half in range(2):
+        gathered[half, me] = x_pad[half * half_rows : (half + 1) * half_rows].astype(bf16)
     pl.semaphore_wait(barrier, n_dev - 1)
 
     def to_peer(source, target, send_sem, recv_sem, step):
@@ -92,21 +95,38 @@
     pair = me + 1 - 2 * lax.rem(me, 2)
     chip_steps = sorted(range(2, n_dev, 2), key=lambda step: -min(step, n_dev - step))
 
-    def block_copy(owner, peer, sem_at):
+    def block_copy(half, owner, peer, sem_at):
         return pltpu.make_async_remote_copy(
-            src_ref=gathered.at[owner],
-            dst_ref=gathered.at[owner],
-            send_sem=gather_send.at[sem_at],
-            recv_sem=gather_recv.at[sem_at],
+            src_ref=gathered.at[half, owner],
+            dst_ref=gathered.at[half, owner],
+            send_sem=gather_send.at[half, sem_at],
+            recv_sem=gather_recv.at[half, sem_at],
             device_id={"aux": peer},
             device_id_type=MESH,
         )
 
-    def direct_copy(step):
-        return block_copy(me, lax.rem(me + step, n_dev), step)
-
-    def passed_copy(step):
-        return block_copy(lax.rem(me + n_dev - step, n_dev), pair, step + 1)
+    def pair_copy(half):
+        return block_copy(half, me, pair, 1)
+
+    def direct_copy(half, step):
+        return block_copy(half, me, lax.rem(me + step, n_dev), step)
+
+    def passed_copy(half, step):
+        return block_copy(half, lax.rem(me + n_dev - step, n_dev), pair, step + 1)
+
+    def pass_on(half):
+        for step in reversed(chip_steps):
+            direct_copy(half, step).wait_recv()
+            passed_copy(half, step).start()
+
+    def take_in(half):
+        pair_copy(half).wait_recv()
+        for step in reversed(chip_steps):
+            passed_copy(half, step).wait_recv()
+        wide = gathered[half].astype(f32).reshape(n_dev, half_trials, rows, width)
+        for n in range(half_trials):
+            at = half * half_trials + n
+            x_t[:, at * n_occ : (at + 1) * n_occ] = wide[:, n].reshape(n_occ, width).T.astype(bf16)
 
     def sum_copy(half, step):
         peer = lax.rem(me + step, n_dev)
@@ -127,19 +147,15 @@
 
         lax.fori_loop(1, n_dev, body, 0)
 
-    for step in chip_steps:
-        direct_copy(step).start()
-    block_copy(me, pair, 1).start()
+    for half in range(2):
+        for step in chip_steps:
+            direct_copy(half, step).start()
+        pair_copy(half).start()
 
     block = 16
     tiles = n_virt // block
     z_rows, z_cols = n_trial * block, aux_local * block
     loads[0].wait()
-    for t in range(tiles):
-        coul_t[t * n_occ : (t + 1) * n_occ, :] = (
-            coul[:, t * block : (t + 1) * block, :].reshape(z_cols, n_occ).T
-        )
-    loads[1].wait()
 
     def turn(index, carry):
         for p in range(group):
@@ -148,19 +164,15 @@
         return carry
 
     lax.fori_loop(0, aux_local // group, turn, 0)
+    loads[1].wait()
+    for t in range(tiles):
+        coul_t[t * n_occ : (t + 1) * n_occ, :] = (
+            coul[:, t * block : (t + 1) * block, :].reshape(z_cols, n_occ).T
+        )
     loads[2].wait()
-    for step in reversed(chip_steps):
-        direct_copy(step).wait_recv()
-        passed_copy(step).start()
-    block_copy(me, pair, 1).wait_recv()
-    for step in reversed(chip_steps):
-        passed_copy(step).wait_recv()
-
-    wide = gathered[...].astype(f32).reshape(n_dev, n_trial, rows, width)
-    for n in range(n_trial):
-        x_t[:, n * n_occ : (n + 1) * n_occ] = (
-            wide[:, n].reshape(n_occ, width).T.astype(bf16)
-        )
+    pass_on(0)
+    take_in(0)
+    total[...] = jnp.zeros_like(total)
 
     def first_step(half, index, slot):
         slot[...] = jnp.dot(
@@ -169,61 +181,58 @@
             preferred_element_type=f32,
         ).astype(bf16)
 
-    first_step(0, 0, halfway_a)
-
-    left = jnp.concatenate(
-        [
-            jnp.concatenate(
-                [
-                    x_t[t * block : (t + 1) * block, n * n_occ : (n + 1) * n_occ]
-                    for n in range(n_trial)
-                ],
-                axis=0,
-            )
-            for t in range(tiles)
-        ],
-        axis=1,
-    )
-    z = jnp.dot(left, coul_t[...], preferred_element_type=f32)
-    same = (
-        lax.broadcasted_iota(jnp.int32, (z_rows, z_cols), 0) % block
-        == lax.broadcasted_iota(jnp.int32, (z_rows, z_cols), 1) % block
-    )
-    z = jnp.sum(jnp.where(same, z, 0.0).reshape(n_trial, block, z_cols), axis=1)
-    lanes = 128
-    chunks = z_cols // lanes
-    ones = (
-        lax.broadcasted_iota(jnp.int32, (lanes, lanes), 0) // block
-        == lax.broadcasted_iota(jnp.int32, (lanes, lanes), 1) // block
-    ).astype(bf16)
-    z = jnp.concatenate([z[:, c * lanes : (c + 1) * lanes] for c in range(chunks)], axis=0)
-    coef = jnp.zeros_like(z)
-    for _ in range(3):
-        piece = z.astype(bf16)
-        z = z - piece.astype(f32)
-        coef = coef + jnp.dot(piece, ones, preferred_element_type=f32)
-    coef = jnp.concatenate(
-        [coef[c * n_trial : (c + 1) * n_trial] for c in range(chunks)], axis=1
-    )
-    coef = jnp.broadcast_to(coef[:, None, :], (n_trial, block, z_cols)).reshape(z_rows, z_cols)
-    spread = jnp.where(same, coef, 0.0).astype(bf16)
-    total[...] = jnp.zeros_like(total)
-    for pair in range(tiles // 2):
-        right = jnp.concatenate(
+    def add_coulomb():
+        left = jnp.concatenate(
             [
-                coul[:, (2 * pair + t) * block : (2 * pair + t + 1) * block, :].reshape(z_cols, n_occ)
-                for t in range(2)
+                jnp.concatenate(
+                    [
+                        x_t[t * block : (t + 1) * block, n * n_occ : (n + 1) * n_occ]
+                        for n in range(n_trial)
+                    ],
+                    axis=0,
+                )
+                for t in range(tiles)
             ],
             axis=1,
         )
-        part = 2.0 * jnp.dot(spread, right, preferred_element_type=f32)
-        for t in range(2):
-            for n in range(n_trial):
-                total[n, (2 * pair + t) * block : (2 * pair + t + 1) * block, :] = part[
-                    n * block : (n + 1) * block, t * n_occ : (t + 1) * n_occ
-                ]
-
-    for half in range(2):
+        z = jnp.dot(left, coul_t[...], preferred_element_type=f32)
+        same = (
+            lax.broadcasted_iota(jnp.int32, (z_rows, z_cols), 0) % block
+            == lax.broadcasted_iota(jnp.int32, (z_rows, z_cols), 1) % block
+        )
+        z = jnp.sum(jnp.where(same, z, 0.0).reshape(n_trial, block, z_cols), axis=1)
+        chunks = z_cols // lanes
+        ones = (
+            lax.broadcasted_iota(jnp.int32, (lanes, lanes), 0) // block
+            == lax.broadcasted_iota(jnp.int32, (lanes, lanes), 1) // block
+        ).astype(bf16)
+        z = jnp.concatenate([z[:, c * lanes : (c + 1) * lanes] for c in range(chunks)], axis=0)
+        coef = jnp.zeros_like(z)
+        for _ in range(3):
+            piece = z.astype(bf16)
+            z = z - piece.astype(f32)
+            coef = coef + jnp.dot(piece, ones, preferred_element_type=f32)
+        coef = jnp.concatenate(
+            [coef[c * n_trial : (c + 1) * n_trial] for c in range(chunks)], axis=1
+        )
+        coef = jnp.broadcast_to(coef[:, None, :], (n_trial, block, z_cols)).reshape(z_rows, z_cols)
+        spread = jnp.where(same, coef, 0.0).astype(bf16)
+        for index in range(tiles // 2):
+            spans = [slice((2 * index + t) * block, (2 * index + t + 1) * block) for t in range(2)]
+            right = jnp.concatenate(
+                [coul[:, span, :].reshape(z_cols, n_occ) for span in spans], axis=1
+            )
+            part = 2.0 * jnp.dot(spread, right, preferred_element_type=f32)
+            for t, span in enumerate(spans):
+                for n in range(n_trial):
+                    total[n, span, :] = (
+                        total[n, span, :]
+                        + part[n * block : (n + 1) * block, t * n_occ : (t + 1) * n_occ]
+                    )
+
+    first_step(0, 0, halfway_a)
+    for half in range(2):
+
         def second_step(index, slot, half=half):
             left = jnp.concatenate(
                 [
@@ -254,12 +263,21 @@
             return carry
 
         groups = aux_local // group
-        lax.fori_loop(0, groups // 2 - 1, exchange, 0)
+        if half == 0:
+            middle = groups // 4
+            lax.fori_loop(0, middle, exchange, 0)
+            pass_on(1)
+            lax.fori_loop(middle, groups // 2 - 1, exchange, 0)
+        else:
+            lax.fori_loop(0, groups // 2 - 1, exchange, 0)
         first_step(half, groups - 1, halfway_b)
         second_step(groups - 2, halfway_a)
         if half == 0:
+            take_in(1)
             first_step(1, 0, halfway_a)
         second_step(groups - 1, halfway_b)
+        if half == 0:
+            add_coulomb()
         outgoing[half] = jnp.concatenate(
             [
                 total[half * half_trials + n].T.reshape(n_dev, rows, width)
@@ -316,10 +334,11 @@
     for n in range(n_trial):
         update_ref[n] = precond[n] * lax.rsqrt(norms[n : n + 1, :1] / count + 1e-06)
 
-    block_copy(me, pair, 1).wait_send()
-    for step in chip_steps:
-        direct_copy(step).wait_send()
-        passed_copy(step).wait_send()
+    for half in range(2):
+        pair_copy(half).wait_send()
+        for step in chip_steps:
+            direct_copy(half, step).wait_send()
+            passed_copy(half, step).wait_send()
     for half in range(2):
         each(lambda step, half=half: sum_copy(half, step).wait_send())
     each(lambda step: scalar_copy(step).wait_send())
@@ -351,7 +370,7 @@
             pltpu.VMEM((aux_local, n_occ, n_occ), jnp.bfloat16),
             pltpu.VMEM((aux_local, n_virt, n_virt), jnp.bfloat16),
             pltpu.VMEM((n_trial * rows, width), jnp.float32),
-            pltpu.VMEM((n_dev, n_trial * rows, width), jnp.bfloat16),
+            pltpu.VMEM((2, n_dev, half_rows, width), jnp.bfloat16),
             pltpu.VMEM((width, n_trial * n_occ), jnp.bfloat16),
             pltpu.VMEM((n_trial, width, n_occ), jnp.float32),
             pltpu.VMEM((2, n_dev, half_rows, width), jnp.bfloat16),
@@ -365,8 +384,8 @@
             pltpu.VMEM((n_virt * n_occ // 16, aux_local * 16), jnp.bfloat16),
             pltpu.VMEM((aux_local * n_occ, n_occ), jnp.bfloat16),
             dma((3,)),
-            dma((n_dev,)),
-            dma((n_dev,)),
+            dma((2, n_dev)),
+            dma((2, n_dev)),
             dma((2, n_dev)),
             dma((2, n_dev)),
             dma((n_dev,)),

time: 39.1 us -> 38.8 us (level)
  no operation moved by 1% of the time
where the time goes in v6:
time: 38.8 us; the launch traced here: 38.6 us
  Pallas kernels  38 us (98%)
  between operations  0.64 us (2%)
    pallas_call x1, Pallas kernels, on_device(): pl.pallas_call(functools.partial(sigma_kernel, n_dev, group), out_shape=(...  36.5 us
    pallas_call x1, Pallas kernels, on_device(): pl.pallas_call(hand_over, out_shape=(out, out), in_specs=[vmem] * 2, out_...  1.4 us

profile of v6, /device:TPU:0, one launch (start us, length us, event | category | flops | bytes accessed | tf_op | source)
XLA Modules:
  0.0 38.6 jit_solution(13067943095277650125)
XLA Ops:
  0.6 36.5 %shard_map.77 = (f32[4,8,224]{2,1,0:T(8,128)}, f32[4,8,224]{2,1,0:T(8,128)}) custom-call(f32[4,8,224]{2,1,0:T(8,128)} %x_ref.1, f32[1,128]{1,0:T(1,128)} %bitcast.5, f32[1,224]{1,0:T(1,128)} %bitcast.4, bf16[64,224,128]{2,1,0:T(8,128)(2,1)} %bitcast.3, bf16[64,128,128]{2,1,0:T(8,128)(2,1)} %oo_hbm.1, bf16[64,224,224]{2,1,0:T(8,128)(2,1)} %vv_hbm.1), custom_call_target="tpu_custom_call" | custom-call | tf_op jit(solution)/shard_map/pallas_call | solution.py:363
  37.2 1.4 %shard_map.78 = (f32[4,8,224]{2,1,0:T(8,128)}, f32[4,8,224]{2,1,0:T(8,128)}) custom-call(f32[4,8,224]{2,1,0:T(8,128)} %get-tuple-element.4.sigma_in, f32[4,8,224]{2,1,0:T(8,128)} %get-tuple-element.5.update_in), custom_call_target="tpu_custom_call" | custom-call | tf_op jit(solution)/shard_map/pallas_call | solution.py:407

commit v7 on v6

--- a/solution.py
+++ b/solution.py
@@ -165,10 +165,6 @@
 
     lax.fori_loop(0, aux_local // group, turn, 0)
     loads[1].wait()
-    for t in range(tiles):
-        coul_t[t * n_occ : (t + 1) * n_occ, :] = (
-            coul[:, t * block : (t + 1) * block, :].reshape(z_cols, n_occ).T
-        )
     loads[2].wait()
     pass_on(0)
     take_in(0)
@@ -263,13 +259,24 @@
             return carry
 
         groups = aux_local // group
+        trips = groups // 2 - 1
         if half == 0:
+            share = -(-tiles // trips)
+
+            def exchange_and_turn(index, carry, exchange=exchange, share=share):
+                for q in range(share):
+                    t = jnp.minimum(index * share + q, tiles - 1)
+                    coul_t[pl.ds(t * n_occ, n_occ), :] = (
+                        coul[:, pl.ds(t * block, block), :].reshape(z_cols, n_occ).T
+                    )
+                return exchange(index, carry)
+
             middle = groups // 4
-            lax.fori_loop(0, middle, exchange, 0)
+            lax.fori_loop(0, middle, exchange_and_turn, 0)
             pass_on(1)
-            lax.fori_loop(middle, groups // 2 - 1, exchange, 0)
+            lax.fori_loop(middle, trips, exchange_and_turn, 0)
         else:
-            lax.fori_loop(0, groups // 2 - 1, exchange, 0)
+            lax.fori_loop(0, trips, exchange, 0)
         first_step(half, groups - 1, halfway_b)
         second_step(groups - 2, halfway_a)
         if half == 0:
@@ -468,6 +475,7 @@
             and n_occ % 128 == 0
             and n_virt % 32 == 0
             and aux_local % 16 == 0
+            and aux_local >= 32
             and n_dev % 2 == 0
         )
         args = (trial_vecs, occ_energy, vir_energy, coul_ov, exch_oo, exch_vv)

time: 38.8 us -> 38.9 us (level)
  no operation moved by 1% of the time
where the time goes in v7:
time: 38.9 us; the launch traced here: 38.6 us
  Pallas kernels  38 us (98%)
  between operations  0.64 us (2%)
    pallas_call x1, Pallas kernels, on_device(): pl.pallas_call(functools.partial(sigma_kernel, n_dev, group), out_shape=(...  36.6 us
    pallas_call x1, Pallas kernels, on_device(): pl.pallas_call(hand_over, out_shape=(out, out), in_specs=[vmem] * 2, out_...  1.4 us

profile of v7, /device:TPU:0, one launch (start us, length us, event | category | flops | bytes accessed | tf_op | source)
XLA Modules:
  0.0 38.6 jit_solution(8603232803002861462)
XLA Ops:
  0.6 36.6 %shard_map.77 = (f32[4,8,224]{2,1,0:T(8,128)}, f32[4,8,224]{2,1,0:T(8,128)}) custom-call(f32[4,8,224]{2,1,0:T(8,128)} %x_ref.1, f32[1,128]{1,0:T(1,128)} %bitcast.5, f32[1,224]{1,0:T(1,128)} %bitcast.4, bf16[64,224,128]{2,1,0:T(8,128)(2,1)} %bitcast.3, bf16[64,128,128]{2,1,0:T(8,128)(2,1)} %oo_hbm.1, bf16[64,224,224]{2,1,0:T(8,128)(2,1)} %vv_hbm.1), custom_call_target="tpu_custom_call" | custom-call | tf_op jit(solution)/shard_map/pallas_call | solution.py:370
  37.2 1.4 %shard_map.78 = (f32[4,8,224]{2,1,0:T(8,128)}, f32[4,8,224]{2,1,0:T(8,128)}) custom-call(f32[4,8,224]{2,1,0:T(8,128)} %get-tuple-element.4.sigma_in, f32[4,8,224]{2,1,0:T(8,128)} %get-tuple-element.5.update_in), custom_call_target="tpu_custom_call" | custom-call | tf_op jit(solution)/shard_map/pallas_call | solution.py:414

commit v8 on v7

--- a/solution.py
+++ b/solution.py
@@ -362,7 +362,7 @@
     aux_local, n_occ, _ = exch_oo.shape
     width = -(-n_virt // 128) * 128
     half_rows = n_trial // 2 * rows
-    group = math.gcd(aux_local // 2, 8)
+    group = math.gcd(aux_local // 2, 4)
     vmem = pl.BlockSpec(memory_space=pltpu.VMEM)
     anywhere = pl.BlockSpec(memory_space=pl.ANY)
     out = jax.ShapeDtypeStruct(trial_vecs.shape, jnp.float32)

time: 38.9 us -> 40.3 us (1.036)
  Pallas kernels: 38 us -> 39.4 us
    pallas_call x1, Pallas kernels: 36.6 us -> 38 us  [on_device(): pl.pallas_call(functools.partial(sigma_kernel, n_dev, group), out_shape=(...]
where the time goes in v8:
time: 40.3 us; the launch traced here: 40 us
  Pallas kernels  39.4 us (98%)
  between operations  0.64 us (2%)
    pallas_call x1, Pallas kernels, on_device(): pl.pallas_call(functools.partial(sigma_kernel, n_dev, group), out_shape=(...  38 us
    pallas_call x1, Pallas kernels, on_device(): pl.pallas_call(hand_over, out_shape=(out, out), in_specs=[vmem] * 2, out_...  1.4 us

profile of v8, /device:TPU:0, one launch (start us, length us, event | category | flops | bytes accessed | tf_op | source)
XLA Modules:
  0.0 40.0 jit_solution(2974059146093192685)
XLA Ops:
  0.6 38.0 %shard_map.77 = (f32[4,8,224]{2,1,0:T(8,128)}, f32[4,8,224]{2,1,0:T(8,128)}) custom-call(f32[4,8,224]{2,1,0:T(8,128)} %x_ref.1, f32[1,128]{1,0:T(1,128)} %bitcast.5, f32[1,224]{1,0:T(1,128)} %bitcast.4, bf16[64,224,128]{2,1,0:T(8,128)(2,1)} %bitcast.3, bf16[64,128,128]{2,1,0:T(8,128)(2,1)} %oo_hbm.1, bf16[64,224,224]{2,1,0:T(8,128)(2,1)} %vv_hbm.1), custom_call_target="tpu_custom_call" | custom-call | tf_op jit(solution)/shard_map/pallas_call | solution.py:370
  38.6 1.4 %shard_map.78 = (f32[4,8,224]{2,1,0:T(8,128)}, f32[4,8,224]{2,1,0:T(8,128)}) custom-call(f32[4,8,224]{2,1,0:T(8,128)} %get-tuple-element.4.sigma_in, f32[4,8,224]{2,1,0:T(8,128)} %get-tuple-element.5.update_in), custom_call_target="tpu_custom_call" | custom-call | tf_op jit(solution)/shard_map/pallas_call | solution.py:414
